TPU v7x, 32 devices: a whole 2x2x4 slice. The times are simulated.
32 devices in a mesh: groups: 2 (over y), sec: 4 (over z), env: 2 (over x), rep: 2 (over core).
Axes of the slice: x: 2, y: 2, z: 4, core: 2. Of those that a mesh axis runs over, the one named last changes fastest.
Arguments:
- wavefunction: bfloat16 [32, 256, 256], P(('groups', 'sec'), None, 'rep'), parts along dimension 0, may hold values from -6 to 6
- left_env: bfloat16 [8, 8, 256, 256], P(('groups', 'env'), 'sec'), parts along dimension 0, may hold values from -0.078125 to 0.078125
- right_env: bfloat16 [8, 16, 256, 256], P(('groups', 'env'), 'sec', 'rep'), parts along dimension 0, may hold values from -0.375 to 0.375
- left_index: int32 [8, 16, 6], P(('groups', 'env'), 'sec'), parts along dimension 0, may hold values from 0 to 7
- out_sector: int32 [8, 16, 6], P(('groups', 'env'), 'sec'), parts along dimension 0, may hold values from 0 to 15, as said below
Outputs:
- product: float32 [32, 256, 256], P(('groups', 'sec'), None, 'rep'), parts along dimension 0
There are 2 independent parts, one for each index of `groups`. A program takes and returns all parts, laid end to end along the dimension named above; each array names one. Nothing has to cross between parts.
Inputs may be any that keep to these rules, and one draw needn't show every extreme that they name: `out_sector`: group the pairs by device: those with terms of one index of env and input sectors of one index of sec. The output sectors named by such a group are 5 distinct ones, of which at most 2 belong to the sectors of any one index of sec, and exactly 2 to some index.
All inputs are finite; a program needn't handle non-finite values.
Results may differ from a plain program's by a relative error of at most 0.0029.
Values may be sent and summed in bfloat16 or wider, within the bound.
A program may use at most 64 MiB of HBM per device.

v0:
```python
import jax
import jax.numpy as jnp
from jax import lax
from jax.sharding import PartitionSpec as P

OUTS = 6
CAP_OUT = 2


def on_device(wavefunction, left_env, right_env, left_index, out_sector):
    sec_count = lax.axis_size("sec")
    full_wave = lax.all_gather(wavefunction, "rep", axis=2, tiled=True)
    half_products = jnp.einsum(
        "sij,ksrj->ksir", full_wave, right_env, preferred_element_type=jnp.float32
    ).astype(jnp.bfloat16)
    dev_terms = half_products.shape[0]
    dev_sectors = half_products.shape[1]
    block_width = half_products.shape[2]
    half_width = half_products.shape[3]
    targets = out_sector.reshape(-1)
    pair_count = targets.shape[0]
    owner_of = targets // dev_sectors
    pair_order = jnp.arange(pair_count)
    earlier = pair_order[None, :] < pair_order[:, None]
    equal_pairs = targets[None, :] == targets[:, None]
    leading = jnp.logical_not(jnp.any(equal_pairs & earlier, axis=1))
    below_mask = (
        leading[None, :]
        & (owner_of[None, :] == owner_of[:, None])
        & (targets[None, :] < targets[:, None])
    )
    slot_rank = jnp.sum(below_mask, axis=1)
    slot_index = owner_of * CAP_OUT + slot_rank
    slot_total = sec_count * CAP_OUT
    labels = jnp.zeros((slot_total,), jnp.int32).at[slot_index].set(targets % dev_sectors)
    per_term = dev_sectors * OUTS
    buffer = jnp.zeros((slot_total, block_width, half_width), jnp.float32)
    all_blocks = lax.all_gather(left_env, "sec", axis=1, tiled=True)
    for term_index in range(dev_terms):
        blocks = all_blocks[term_index]
        picked = blocks[left_index[term_index].reshape(-1)].reshape(
            dev_sectors, OUTS, block_width, block_width
        )
        partial_blocks = jnp.einsum(
            "smij,sjl->smil", picked, half_products[term_index], preferred_element_type=jnp.float32
        )
        partial_blocks = partial_blocks.reshape(per_term, block_width, half_width)
        term_slots = slot_index[term_index * per_term : (term_index + 1) * per_term]
        buffer = buffer + jax.ops.segment_sum(partial_blocks, term_slots, num_segments=slot_total)
    received, slot_labels = (
        lax.all_to_all(
            buffer.reshape(sec_count, CAP_OUT, block_width, half_width),
            "sec",
            split_axis=0,
            concat_axis=0,
            tiled=True,
        ),
        lax.all_to_all(
            labels.reshape(sec_count, CAP_OUT), "sec", split_axis=0, concat_axis=0, tiled=True
        ),
    )
    owned_sums = jax.ops.segment_sum(
        received.reshape(-1, block_width, half_width),
        slot_labels.reshape(-1),
        num_segments=dev_sectors,
    )
    return lax.psum(owned_sums, "env")


def solution(mesh):
    in_specs = (
        P(("groups", "sec"), None, "rep"),
        P(("groups", "env"), "sec", None, None),
        P(("groups", "env"), "sec", "rep", None),
        P(("groups", "env"), "sec", None),
        P(("groups", "env"), "sec", None),
    )
    out_specs = P(("groups", "sec"), None, "rep")
    return jax.shard_map(
        on_device, mesh=mesh, in_specs=in_specs, out_specs=out_specs, check_vma=False
    )
```

profile of v0, /device:TPU:0, one launch (start us, length us, event | category | flops | bytes accessed | tf_op | source)
XLA Modules:
  0.0 153.3 jit_solution(16452875529927064882)
XLA Ops:
  6.5 0.7 all-gather.2.cloned.1.call-update
  7.3 0.8 eq.30
  8.0 0.8 reshape.213
  9.2 0.7 scatter_custom_fusion
  9.9 0.7 all_to_all.9
  10.6 6.3 %all-to-all-start = ((s32[4,1,2]{2,1,0:T(1,128)}), s32[4,1,2]{2,1,0:T(1,128)S(1)}, u32[]{:S(2)}, u32[]{:S(2)}) async-start(s32[4,1,2]{2,1,0:T(1,128)} %bitcast.2), calls=%async_computation | async-start | bytes 4096 | tf_op jit(solution)/shard_map/all_to_all | solution.py:58
  16.9 0.7 fusion.12
  17.8 2.4 %all_gather.7 = bf16[4,256,256]{2,1,0:T(8,128)(2,1)S(1)} all-gather(bf16[4,256,128]{2,1,0:T(8,128)(2,1)} %param.5), channel_id=1, replica_groups=mesh['groups'=2,'sec'=4,'env'=2,'rep'=2] {'rep'}, dimensions={2}, use_global_device_ids=true | all-gather | bytes 786432 | tf_op jit(solution)/shard_map/all_gather | solution.py:12
  20.3 2.2 %fusion = bf16[2,4,256,128]{2,3,0,1:T(8,128)(2,1)} fusion(bf16[4,256,256]{2,1,0:T(8,128)(2,1)S(1)} %all_gather.7, bf16[2,4,128,256]{3,2,1,0:T(8,128)(2,1)} %param.7), kind=kOutput, calls=%fused_computation.7 | convolution fusion | flops 134479872 | bytes 1572864 | tf_op jit(solution)/shard_map/sij,ksrj->ksir/dot_general | solution.py:13
  22.5 35.0 %all-gather.2.cloned.1.call-done = bf16[2,8,256,256]{3,2,1,0:T(8,128)(2,1)} async-done(((bf16[2,2,256,256]{3,2,1,0:T(8,128)(2,1)}), bf16[2,8,256,256]{3,2,1,0:T(8,128)(2,1)}) %all-gather.2.cloned.1.call-update) | async-done | bytes 2097168 | tf_op jit(solution)/shard_map/all_gather | solution.py:38
  57.4 3.0 %slice_bitcast_fusion = (bf16[8,256,256]{2,1,0:T(8,128)(2,1)}, bf16[8,256,256]{2,1,0:T(8,128)(2,1)}) fusion(bf16[2,8,256,256]{3,2,1,0:T(8,128)(2,1)} %all-gather.2.cloned.1.call-done), kind=kLoop, calls=%fused_computation.8 | loop fusion | bytes 4194304 | tf_op jit(solution)/shard_map/squeeze | solution.py:40
  60.5 2.0 %gather_fusion = bf16[24,256,256]{2,1,0:T(8,128)(2,1)S(1)} fusion(bf16[8,256,256]{2,1,0:T(8,128)(2,1)} %get-tuple-element.6, s32[1024]{0:T(1024)S(1)} %pad_clamp_fusion.1), kind=kCustom, calls=%fused_computation | custom fusion | bytes 6291552 | tf_op jit(solution)/shard_map/gather | solution.py:41
  62.4 3.6 %fusion.4 = f32[4,6,256,128]{3,2,1,0:T(8,128)} fusion(bf16[4,6,256,256]{3,2,1,0:T(8,128)(2,1)S(1)} %bitcast.45, bf16[2,4,256,128]{2,3,0,1:T(8,128)(2,1)} %fusion), kind=kOutput, calls=%fused_computation.15 | convolution fusion | flops 402653184 | bytes 6553600 | tf_op jit(solution)/shard_map/smij,sjl->smil/dot_general | solution.py:44
  66.0 2.0 %gather_fusion.1 = bf16[24,256,256]{2,1,0:T(8,128)(2,1)S(1)} fusion(bf16[8,256,256]{2,1,0:T(8,128)(2,1)} %get-tuple-element.5, s32[1024]{0:T(1024)S(1)} %pad_clamp_fusion), kind=kCustom, calls=%fused_computation.1 | custom fusion | bytes 6291552 | tf_op jit(solution)/shard_map/gather | solution.py:41
  68.0 3.6 %fusion.3 = f32[4,6,256,128]{3,2,1,0:T(8,128)} fusion(bf16[4,6,256,256]{3,2,1,0:T(8,128)(2,1)S(1)} %bitcast.44, bf16[2,4,256,128]{2,3,0,1:T(8,128)(2,1)} %fusion), kind=kOutput, calls=%fused_computation.13 | convolution fusion | flops 402653184 | bytes 6553600 | tf_op jit(solution)/shard_map/smij,sjl->smil/dot_general | solution.py:44
  71.7 6.1 %scatter_fusion = f32[8,256,128]{2,1,0:T(8,128)S(1)} fusion(f32[8,256,128]{2,1,0:T(8,128)S(1)} %broadcast.164.clone, s32[24]{0:T(128)S(1)} %get-tuple-element.10, f32[24,256,128]{2,1,0:T(8,128)} %bitcast.46), kind=kCustom, calls=%fused_computation.3 | custom fusion | flops 786432 | bytes 9437280 | tf_op jit(solution)/shard_map/scatter-add | solution.py:49
  77.9 6.1 %scatter_fusion.1 = f32[8,256,128]{2,1,0:T(8,128)S(1)} fusion(f32[8,256,128]{2,1,0:T(8,128)S(1)} %broadcast.164.clone.1, s32[24]{0:T(128)S(1)} %get-tuple-element.9, f32[24,256,128]{2,1,0:T(8,128)} %bitcast.47), kind=kCustom, calls=%fused_computation.4 | custom fusion | flops 786432 | bytes 9437280 | tf_op jit(solution)/shard_map/scatter-add | solution.py:49
  83.9 1.1 add.84
  85.0 3.5 %all-to-all-start.1 = ((f32[4,2,256,128]{3,2,1,0:T(8,128)}), f32[4,2,256,128]{3,2,1,0:T(8,128)S(1)}, u32[]{:S(2)}, u32[]{:S(2)}) async-start(f32[4,2,256,128]{3,2,1,0:T(8,128)} %bitcast.18), calls=%async_computation.1 | async-start | bytes 2097152 | tf_op jit(solution)/shard_map/all_to_all | solution.py:51
  89.9 24.6 %all-to-all-done.1 = f32[4,2,256,128]{3,2,1,0:T(8,128)S(1)} async-done(((f32[4,2,256,128]{3,2,1,0:T(8,128)}), f32[4,2,256,128]{3,2,1,0:T(8,128)S(1)}, u32[]{:S(2)}, u32[]{:S(2)}) %all-to-all-start.1) | async-done | bytes 1048608 | tf_op jit(solution)/shard_map/all_to_all | solution.py:51
  114.5 1.3 scatter_fusion.2
  115.9 0.8 copy-done
  116.7 28.0 %all-reduce.2.cloned.1.call-done = f32[4,256,128]{2,1,0:T(8,128)} async-done(((f32[4,256,128]{2,1,0:T(8,128)}), f32[4,256,128]{2,1,0:T(8,128)}) %all-reduce.2.cloned.1.call-update) | async-done | bytes 524304 | tf_op jit(solution)/shard_map/psum | solution.py:67
  144.6 1.9 %copy.33 = f32[4,256,128]{2,1,0:T(8,128)} copy(f32[4,256,128]{2,1,0:T(8,128)} %all-reduce.2.cloned.1.call-done) | data formatting | bytes 1048576
  (24 shorter events, 2.2 us)
Async XLA Ops:
  6.5 50.9 %all-gather.2.cloned.1.call-start = ((), (), s32[]{:S(2)}) async-start(), calls=%async_computation.2 | async-start | bytes 2621440 | tf_op jit(solution)/shard_map/all_gather | solution.py:38
  10.6 74.4 %all-to-all-start = ((s32[4,1,2]{2,1,0:T(1,128)}), s32[4,1,2]{2,1,0:T(1,128)S(1)}, u32[]{:S(2)}, u32[]{:S(2)}) async-start(s32[4,1,2]{2,1,0:T(1,128)} %bitcast.2), calls=%async_computation | async-start | bytes 4096 | tf_op jit(solution)/shard_map/all_to_all | solution.py:58
  85.0 29.4 %all-to-all-start.1 = ((f32[4,2,256,128]{3,2,1,0:T(8,128)}), f32[4,2,256,128]{3,2,1,0:T(8,128)S(1)}, u32[]{:S(2)}, u32[]{:S(2)}) async-start(f32[4,2,256,128]{3,2,1,0:T(8,128)} %bitcast.18), calls=%async_computation.1 | async-start | bytes 2097152 | tf_op jit(solution)/shard_map/all_to_all | solution.py:51
  88.6 56.1 %all-reduce.2.cloned.1.call-start = ((), (), s32[]{:S(2)}) async-start(), calls=%async_computation.3 | async-start | bytes 1048576 | tf_op jit(solution)/shard_map/psum | solution.py:67
  115.8 0.8 copy-start
Sparse Core Ops, SparseCore 0:
  8.9 48.4 all-gather.1
  116.8 27.7 all-reduce.1
where the time goes:
time: 154 us; the launch traced here: 153 us
  waiting for transfers between devices  88.2 us (57%)
  other arithmetic  15.6 us (10%)
  local copies, waits for them, and re-layouts  14.3 us (9%)
  between operations  13.5 us (9%)
  starting transfers between devices  9.88 us (6%)
  matrix products  9.4 us (6%)
  blocking collectives  2.39 us (2%)
    all_gather x1, waiting for transfers between devices, on_device(): all_blocks = lax.all_gather(left_env, 'sec', axis=1, tiled=True)  35 us
    psum x1, waiting for transfers between devices, on_device(): return lax.psum(owned_sums, 'env')  28 us
    all_to_all x1, waiting for transfers between devices, on_device(): lax.all_to_all(buffer.reshape(sec_count, CAP_OUT, block_width, half_width...  24.6 us
    scatter-add x2, other arithmetic, on_device(): jax.ops.segment_sum(partial_blocks, term_slots, num_segments=slot_total)  12.1 us
    dot_general x2, matrix products, on_device(): jnp.einsum('smij,sjl->smil', picked, half_products[term_index], preferred...  7.24 us
    all_to_all x1, starting transfers between devices, on_device(): lax.all_to_all(labels.reshape(sec_count, CAP_OUT), 'sec', split_axis=0, c...  6.32 us
    gather x2, local copies, waits for them, and re-layouts, on_device(): blocks[left_index[term_index].reshape(-1)]  3.94 us
    all_to_all x1, starting transfers between devices, on_device(): lax.all_to_all(buffer.reshape(sec_count, CAP_OUT, block_width, half_width...  3.52 us
  transfers between devices with their start and end apart: 4, of which 3 were waited for; matrix products, arithmetic and copies ran while one was open for 23% of the time, Pallas kernels for 0%

commit v1 on v0

v1 whole, which is shorter than its diff:
```python
import functools

import jax
import jax.numpy as jnp
from jax import lax
from jax.experimental import pallas as pl
from jax.experimental.pallas import tpu as pltpu
from jax.sharding import PartitionSpec as P

MESH = pl.DeviceIdType.MESH
SLOTS = 2
CHUNKS = 1


def kernel(dims, *refs):
    n, n_env, chunks, terms, sectors, blocks, outs = dims
    wave_ref, left_ref, right_ref, lidx_ref, osec_ref, out_ref = refs[:6]
    refs = list(refs[6:])
    wave_all, prods, chain, lab_send, lab_recv, dense_own, prev_s, last_s = refs[:8]
    refs = refs[8:]
    left_all = refs[:chunks]
    slot_send = refs[chunks : 2 * chunks]
    slot_recv = refs[2 * chunks : 3 * chunks]
    env_all = refs[3 * chunks : 4 * chunks]
    (up_s, up_r, dn_s, dn_r, sib_s, sib_r, w_s, w_r, sl_s, sl_r, lb_s, lb_r, ev_s, ev_r, loc) = refs[4 * chunks :]
    me = lax.axis_index("sec")
    env = lax.axis_index("env")
    core = lax.axis_index("rep")
    per = terms * blocks
    pairs = terms * sectors * outs
    rows = left_ref.shape[2] * left_ref.shape[3]
    width = wave_ref.shape[-1]

    barrier = pltpu.get_barrier_semaphore()
    for d in range(1, n):
        pl.semaphore_signal(barrier, inc=1, device_id={"sec": lax.rem(me + d, n)}, device_id_type=MESH)
    for d in range(1, n_env):
        pl.semaphore_signal(barrier, inc=1, device_id={"env": lax.rem(env + d, n_env)}, device_id_type=MESH)
    pl.semaphore_signal(barrier, inc=1, device_id={"rep": 1 - core}, device_id_type=MESH)
    pl.semaphore_wait(barrier, n - 1 + n_env - 1 + 1)

    def remote(src, dst, send, recv, where):
        return pltpu.make_async_remote_copy(
            src_ref=src, dst_ref=dst, send_sem=send, recv_sem=recv, device_id=where, device_id_type=MESH
        )

    def piece(r, origin):
        return left_all[r].at[pl.ds(origin * per, per), core]

    def hop(r, s, up, origin):
        src = left_ref.at[:, r, core] if s == 0 else piece(r, origin)
        send, recv = (up_s, up_r) if up else (dn_s, dn_r)
        where = jnp.minimum(me + 1, n - 1) if up else jnp.maximum(me - 1, 0)
        return remote(src, piece(r, origin), send.at[r, s], recv.at[r, s], {"sec": where})

    def sibling(r, origin, half):
        ref = left_all[r].at[pl.ds(origin * per, per), half]
        return remote(ref, ref, sib_s.at[r, origin], sib_r.at[r, origin], {"rep": 1 - core})

    def begin(r):
        @pl.when(me + 1 < n)
        def _():
            hop(r, 0, True, me).start()

        @pl.when(me > 0)
        def _():
            hop(r, 0, False, me).start()

    def relay(r):
        for s in range(n - 1):
            @pl.when(me - 1 - s >= 0)
            def _():
                origin = me - 1 - s
                hop(r, s, True, origin).wait_recv()
                if s + 1 <= n - 2:
                    @pl.when(me + 1 < n)
                    def _():
                        hop(r, s + 1, True, origin).start()
                sibling(r, origin, core).start()

            @pl.when(me + 1 + s <= n - 1)
            def _():
                origin = me + 1 + s
                hop(r, s, False, origin).wait_recv()
                if s + 1 <= n - 2:
                    @pl.when(me > 0)
                    def _():
                        hop(r, s + 1, False, origin).start()
                sibling(r, origin, core).start()

    def gathered(r):
        for d in range(1, n):
            sibling(r, lax.rem(me + d, n), 1 - core).wait_recv()

    begin(0)
    wave_copy = remote(wave_ref, wave_all.at[core], w_s, w_r, {"rep": 1 - core})
    wave_copy.start()
    own_copies = [
        pltpu.make_async_copy(left_ref.at[:, r], left_all[r].at[pl.ds(me * per, per)], loc.at[r])
        for r in range(chunks)
    ]
    for copy in own_copies:
        copy.start()
    wave_all[core] = wave_ref[...]

    def find_prev(p, carry):
        target = osec_ref[p]
        found = jnp.int32(pairs)
        for q in range(pairs - 1):
            found = jnp.where((osec_ref[q] == target) & (q < p), q, found)
        prev_s[p] = found
        return carry

    lax.fori_loop(0, pairs, find_prev, 0)

    def find_last(v, carry):
        found = jnp.int32(-1)
        for q in range(pairs):
            found = jnp.where(osec_ref[q] == v, q, found)
        last_s[v] = found
        return carry

    lax.fori_loop(0, n * sectors, find_last, 0)

    def slot_of(owner, i):
        low, high = jnp.int32(-1), jnp.int32(-1)
        for l in range(sectors):
            here = last_s[owner * sectors + l] >= 0
            high = jnp.where(here, l, high)
            low = jnp.where(here & (low < 0), l, low)
        label = low if i == 0 else jnp.where(high == low, -1, high)
        source = jnp.where(label >= 0, last_s[owner * sectors + jnp.maximum(label, 0)], pairs)
        return label, source

    def write_labels(owner, carry):
        for i in range(SLOTS):
            lab_send[owner, i] = jnp.full((8, 128), slot_of(owner, i)[0], jnp.int32)
        return carry

    lax.fori_loop(0, n, write_labels, 0)

    def label_copy(d):
        owner = lax.rem(me + d, n)
        return remote(lab_send.at[owner], lab_recv.at[me], lb_s.at[d], lb_r.at[d], {"sec": owner})

    for d in range(1, n):
        label_copy(d).start()
    wave_copy.wait()

    for s in range(sectors):
        wave = jnp.concatenate([wave_all[0, s], wave_all[1, s]], axis=-1)
        for k in range(terms):
            prods[k * sectors + s] = lax.dot_general(
                wave, right_ref[k, s], (((1,), (1,)), ((), ())), preferred_element_type=jnp.float32
            ).astype(jnp.bfloat16)
    chain[pairs] = jnp.zeros((rows, width), jnp.float32)

    def compute(r):
        def body(ks, carry):
            k = ks // sectors
            right = prods[ks]
            for m in range(outs):
                p = ks * outs + m
                b = lidx_ref[p]
                left = left_all[r][(b // blocks) * per + k * blocks + lax.rem(b, blocks)]
                value = jnp.dot(left.reshape(rows, -1), right, preferred_element_type=jnp.float32)
                chain[p] = value + chain[prev_s[p]]
            return carry

        lax.fori_loop(0, terms * sectors, body, 0)

    def slot_copy(r, d):
        owner = lax.rem(me + d, n)
        return remote(
            slot_send[r].at[pl.ds(owner * SLOTS, SLOTS)],
            slot_recv[r].at[pl.ds(me * SLOTS, SLOTS)],
            sl_s.at[r, d],
            sl_r.at[r, d],
            {"sec": owner},
        )

    def send_slots(r):
        for d in range(n - 1, 0, -1):
            owner = lax.rem(me + d, n)
            for i in range(SLOTS):
                slot_send[r][owner * SLOTS + i] = chain[slot_of(owner, i)[1]].astype(jnp.bfloat16)
            slot_copy(r, d).start()
        labels = [slot_of(me, i) for i in range(SLOTS)]
        parts = [chain[source] for _, source in labels]
        for l in range(sectors):
            total = jnp.zeros((rows, width), jnp.float32)
            for i in range(SLOTS):
                total = total + jnp.where(labels[i][0] == l, parts[i], 0.0)
            dense_own[r, l] = total

    def env_copy(r, d):
        peer = lax.rem(env + d, n_env)
        ref = env_all[r].at[env]
        return remote(ref, ref, ev_s.at[r, d], ev_r.at[r, d], {"env": peer})

    def sum_slots(r):
        for d in range(1, n):
            slot_copy(r, d).wait_recv()
        for l in range(sectors):
            total = dense_own[r, l]
            for d in range(1, n):
                source = lax.rem(me + d, n)
                for i in range(SLOTS):
                    mask = lab_recv[source, i][:1] == l
                    total = total + jnp.where(mask, slot_recv[r][source * SLOTS + i].astype(jnp.float32), 0.0)
            env_all[r][env, l] = total.astype(env_all[r].dtype)
        for d in range(1, n_env):
            env_copy(r, d).start()

    def finish(r):
        for d in range(1, n_env):
            env_copy(r, d).wait_recv()
        for l in range(sectors):
            total = env_all[r][0, l].astype(jnp.float32)
            for e in range(1, n_env):
                total = total + env_all[r][e, l].astype(jnp.float32)
            out_ref[l, r * rows : (r + 1) * rows] = total

    for r in range(chunks):
        relay(r)
        if r + 1 < chunks:
            begin(r + 1)
        gathered(r)
        own_copies[r].wait()
        compute(r)
        send_slots(r)
        if r == 1:
            for d in range(1, n):
                label_copy(d).wait_recv()
        if r >= 1:
            sum_slots(r - 1)
        if r >= 2:
            finish(r - 2)
    if chunks == 1:
        for d in range(1, n):
            label_copy(d).wait_recv()
    sum_slots(chunks - 1)
    for r in range(max(chunks - 2, 0), chunks):
        finish(r)

    for r in range(chunks):
        for s in range(n - 1):
            @pl.when((me - s >= 0) & (me + 1 < n))
            def _():
                hop(r, s, True, me - s).wait_send()

            @pl.when((me + s <= n - 1) & (me > 0))
            def _():
                hop(r, s, False, me + s).wait_send()
        for d in range(1, n):
            sibling(r, lax.rem(me + d, n), core).wait_send()
            slot_copy(r, d).wait_send()
        for d in range(1, n_env):
            env_copy(r, d).wait_send()
    for d in range(1, n):
        label_copy(d).wait_send()


def on_device(n, n_env, wavefunction, left_env, right_env, left_index, out_sector):
    sectors, height, width = wavefunction.shape
    terms, blocks = left_env.shape[:2]
    outs = left_index.shape[-1]
    chunks = CHUNKS
    rows = height // chunks
    pairs = terms * sectors * outs
    per = terms * blocks
    bf16, f32 = jnp.bfloat16, jnp.float32
    left = left_env.reshape(per, chunks, 2, rows // 2, height)
    vmem = pl.BlockSpec(memory_space=pltpu.VMEM)
    smem = pl.BlockSpec(memory_space=pltpu.SMEM)
    dma = pltpu.SemaphoreType.DMA
    scratch = [
        pltpu.VMEM((2, sectors, height, width), bf16),
        pltpu.VMEM((terms * sectors, height, width), bf16),
        pltpu.VMEM((pairs + 1, rows, width), f32),
        pltpu.VMEM((n, SLOTS, 8, 128), jnp.int32),
        pltpu.VMEM((n, SLOTS, 8, 128), jnp.int32),
        pltpu.VMEM((chunks, sectors, rows, width), f32),
        pltpu.SMEM((pairs,), jnp.int32),
        pltpu.SMEM((n * sectors,), jnp.int32),
    ]
    scratch += [pltpu.VMEM((n * per, 2, rows // 2, height), bf16)] * chunks
    scratch += [pltpu.VMEM((n * SLOTS, rows, width), bf16)] * (2 * chunks)
    scratch += [pltpu.VMEM((n_env, sectors, rows, width), bf16)] * chunks
    scratch += [dma((chunks, n - 1))] * 4 + [dma((chunks, n))] * 2 + [dma, dma]
    scratch += [dma((chunks, n))] * 2 + [dma((n,))] * 2 + [dma((chunks, n_env))] * 2 + [dma((chunks,))]
    dims = (n, n_env, chunks, terms, sectors, blocks, outs)
    return pl.pallas_call(
        functools.partial(kernel, dims),
        out_shape=jax.ShapeDtypeStruct(wavefunction.shape, f32),
        in_specs=[vmem, vmem, vmem, smem, smem],
        out_specs=vmem,
        scratch_shapes=scratch,
        compiler_params=pltpu.CompilerParams(
            collective_id=0, has_side_effects=True, vmem_limit_bytes=48 * 1024 * 1024
        ),
    )(wavefunction, left, right_env, left_index.reshape(-1), out_sector.reshape(-1))


def solution(mesh):
    in_specs = (
        P(("groups", "sec"), None, "rep"),
        P(("groups", "env"), "sec", None, None),
        P(("groups", "env"), "sec", "rep", None),
        P(("groups", "env"), "sec", None),
        P(("groups", "env"), "sec", None),
    )
    out_specs = P(("groups", "sec"), None, "rep")
    return jax.shard_map(
        functools.partial(on_device, mesh.shape["sec"], mesh.shape["env"]),
        mesh=mesh,
        in_specs=in_specs,
        out_specs=out_specs,
        check_vma=False,
    )
```

time: 154 us -> 55.7 us (0.36)
  waiting for transfers between devices: 88.2 us -> 0 us
  Pallas kernels: 0 us -> 50.7 us
  other arithmetic: 15.6 us -> 0 us
  between operations: 13.5 us -> 0.01 us
  starting transfers between devices: 9.88 us -> 0 us
  local copies, waits for them, and re-layouts: 14.3 us -> 4.7 us
  matrix products: 9.4 us -> 0 us
  blocking collectives: 2.39 us -> 0 us
    pallas_call x0 -> x1, Pallas kernels: none -> 50.7 us  [on_device(): pl.pallas_call(functools.partial(kernel, dims), out_shape=jax.ShapeDtypeS...]
    all_gather x1 -> x0, waiting for transfers between devices: 35 us -> none  [on_device(): all_blocks = lax.all_gather(left_env, 'sec', axis=1, tiled=True)]
    psum x1 -> x0, waiting for transfers between devices: 28 us -> none  [on_device(): return lax.psum(owned_sums, 'env')]
    all_to_all x2 -> x0, waiting for transfers between devices: 24.6 us -> none  [the longest x1 24.6 us: on_device(): lax.all_to_all(buffer.reshape(sec_count, CAP_OUT, block_width, half_width...]
    scatter-add x3 -> x0, other arithmetic: 13.4 us -> none  [the longest x2 12.1 us: on_device(): jax.ops.segment_sum(partial_blocks, term_slots, num_segments=slot_total)]
    all_to_all x2 -> x0, starting transfers between devices: 9.83 us -> none  [the longest x1 6.32 us: on_device(): lax.all_to_all(labels.reshape(sec_count, CAP_OUT), 'sec', split_axis=0, c...]
    dot_general x3 -> x0, matrix products: 9.4 us -> none  [the longest x2 7.24 us: on_device(): jnp.einsum('smij,sjl->smil', picked, half_products[term_index], preferred...]
    gather x2 -> x0, local copies, waits for them, and re-layouts: 3.94 us -> none  [on_device(): blocks[left_index[term_index].reshape(-1)]]
  transfers between devices with their start and end apart: 4 -> 0, of which waited for: 3 -> 0; matrix products, arithmetic and copies ran while one was open for 23% -> 0% of each run, Pallas kernels for 0% -> 0%
where the time goes in v1:
time: 55.7 us; the launch traced here: 55.4 us
  Pallas kernels  50.7 us (91%)
  local copies, waits for them, and re-layouts  4.7 us (8%)
    pallas_call x1, Pallas kernels, on_device(): pl.pallas_call(functools.partial(kernel, dims), out_shape=jax.ShapeDtypeS...  50.7 us
    unnamed x9, local copies, waits for them, and re-layouts  3.84 us

profile of v1, /device:TPU:0, one launch (start us, length us, event | category | flops | bytes accessed | tf_op | source)
XLA Modules:
  0.0 55.4 jit_solution(12232810959983769194)
XLA Ops:
  0.0 0.0 copy-start.3
  0.0 0.8 %reshape.10.refs_3_ = s32[48]{0:T(128)S(1)} reshape(s32[2,4,6]{2,1,0:T(4,128)} %param.8) | data formatting | bytes 384 | tf_op jit(solution)/shard_map/reshape | solution.py:302
  0.8 0.0 copy-done.3
  0.8 0.1 reshape.11.refs_4_
  0.9 0.0 copy-start
  0.9 1.0 %copy-done = bf16[2,2,256,256]{3,2,1,0:T(8,128)(2,1)S(1)} copy-done((bf16[2,2,256,256]{3,2,1,0:T(8,128)(2,1)S(1)}, bf16[2,2,256,256]{3,2,1,0:T(8,128)(2,1)}, u32[]{:S(2)}) %copy-start) | copy-done | bytes 524312
  1.9 0.0 copy-start.1
  1.9 1.0 %copy-done.1 = bf16[2,4,128,256]{3,2,1,0:T(8,128)(2,1)S(1)} copy-done((bf16[2,4,128,256]{3,2,1,0:T(8,128)(2,1)S(1)}, bf16[2,4,128,256]{3,2,1,0:T(8,128)(2,1)}, u32[]{:S(2)}) %copy-start.1) | copy-done | bytes 524312
  3.0 0.0 copy-start.2
  3.0 0.9 %copy-done.2 = bf16[4,256,128]{2,1,0:T(8,128)(2,1)S(1)} copy-done((bf16[4,256,128]{2,1,0:T(8,128)(2,1)S(1)}, bf16[4,256,128]{2,1,0:T(8,128)(2,1)}, u32[]{:S(2)}) %copy-start.2) | copy-done | bytes 262168
  3.9 50.7 %shard_map.55 = f32[4,256,128]{2,1,0:T(8,128)S(1)} custom-call(bf16[4,256,128]{2,1,0:T(8,128)(2,1)S(1)} %copy-done.2, bf16[4,1,2,128,256]{4,3,2,1,0:T(8,128)(2,1)S(1)} %bitcast.1, bf16[2,4,128,256]{3,2,1,0:T(8,128)(2,1)S(1)} %copy-done.1, s32[48]{0:T(128)S(1)} %reshape.10.refs_3_, s32[48]{0:T(128)S(1)} %reshape.11.refs_4_), custom_call_target="tpu_custom_call" | custom-call | tf_op jit(solution)/shard_map/pallas_call | solution.py:293
  54.6 0.8 %copy.7 = f32[4,256,128]{2,1,0:T(8,128)} copy(f32[4,256,128]{2,1,0:T(8,128)S(1)} %shard_map.55) | data formatting | bytes 1048576
Async XLA Ops:
  0.0 0.8 %copy-start.3 = (s32[2,4,6]{2,1,0:T(4,128)S(1)}, s32[2,4,6]{2,1,0:T(4,128)}, u32[]{:S(2)}) copy-start(s32[2,4,6]{2,1,0:T(4,128)} %param.9) | copy-start | bytes 580
  0.9 1.0 %copy-start = (bf16[2,2,256,256]{3,2,1,0:T(8,128)(2,1)S(1)}, bf16[2,2,256,256]{3,2,1,0:T(8,128)(2,1)}, u32[]{:S(2)}) copy-start(bf16[2,2,256,256]{3,2,1,0:T(8,128)(2,1)} %param.6) | copy-start | bytes 1572868
  1.9 1.0 %copy-start.1 = (bf16[2,4,128,256]{3,2,1,0:T(8,128)(2,1)S(1)}, bf16[2,4,128,256]{3,2,1,0:T(8,128)(2,1)}, u32[]{:S(2)}) copy-start(bf16[2,4,128,256]{3,2,1,0:T(8,128)(2,1)} %refs_2_.1) | copy-start | bytes 1572868
  3.0 0.9 %copy-start.2 = (bf16[4,256,128]{2,1,0:T(8,128)(2,1)S(1)}, bf16[4,256,128]{2,1,0:T(8,128)(2,1)}, u32[]{:S(2)}) copy-start(bf16[4,256,128]{2,1,0:T(8,128)(2,1)} %refs_0_.1) | copy-start | bytes 786436

commit v2 on v1

--- a/solution.py
+++ b/solution.py
@@ -10,25 +10,28 @@
 MESH = pl.DeviceIdType.MESH
 SLOTS = 2
 CHUNKS = 1
+PARTS = 4
 
 
 def kernel(dims, *refs):
-    n, n_env, chunks, terms, sectors, blocks, outs = dims
-    wave_ref, left_ref, right_ref, lidx_ref, osec_ref, out_ref = refs[:6]
+    n, n_env, chunks, parts, terms, sectors, blocks, outs = dims
+    units = chunks * parts
+    wave_ref, left_ref, right_hbm, lidx_in, osec_in, out_ref = refs[:6]
     refs = list(refs[6:])
-    wave_all, prods, chain, lab_send, lab_recv, dense_own, prev_s, last_s = refs[:8]
-    refs = refs[8:]
+    wave_all, right_ref, prods, chain, lab_send, lab_recv, dense_own, prev_s, last_s, lidx_s, osec_s, lidx_ref, osec_ref = refs[:13]
+    refs = refs[13:]
     left_all = refs[:chunks]
-    slot_send = refs[chunks : 2 * chunks]
-    slot_recv = refs[2 * chunks : 3 * chunks]
-    env_all = refs[3 * chunks : 4 * chunks]
-    (up_s, up_r, dn_s, dn_r, sib_s, sib_r, w_s, w_r, sl_s, sl_r, lb_s, lb_r, ev_s, ev_r, loc) = refs[4 * chunks :]
+    refs = refs[chunks:]
+    slot_send = refs[:units]
+    slot_recv = refs[units : 2 * units]
+    env_all = refs[2 * units : 3 * units]
+    (up_s, up_r, dn_s, dn_r, sib_s, sib_r, w_s, w_r, sl_s, sl_r, lb_s, lb_r, ev_s, ev_r, loc) = refs[3 * units :]
     me = lax.axis_index("sec")
     env = lax.axis_index("env")
     core = lax.axis_index("rep")
     per = terms * blocks
     pairs = terms * sectors * outs
-    rows = left_ref.shape[2] * left_ref.shape[3]
+    rows = left_ref.shape[2] * left_ref.shape[3] // parts
     width = wave_ref.shape[-1]
 
     barrier = pltpu.get_barrier_semaphore()
@@ -101,7 +104,22 @@
     ]
     for copy in own_copies:
         copy.start()
-    wave_all[core] = wave_ref[...]
+    in_copies = [
+        pltpu.make_async_copy(wave_ref, wave_all.at[core], loc.at[chunks]),
+        pltpu.make_async_copy(right_hbm, right_ref, loc.at[chunks + 1]),
+    ]
+    index_copies = [
+        pltpu.make_async_copy(lidx_in, lidx_s, loc.at[chunks + 2]),
+        pltpu.make_async_copy(osec_in, osec_s, loc.at[chunks + 3]),
+    ]
+    for copy in index_copies + in_copies:
+        copy.start()
+    for copy in index_copies:
+        copy.wait()
+    for p in range(pairs):
+        k, s, m = p // (sectors * outs), p // outs % sectors, p % outs
+        lidx_ref[p] = lidx_s[k, s, m]
+        osec_ref[p] = osec_s[k, s, m]
 
     def find_prev(p, carry):
         target = osec_ref[p]
@@ -146,6 +164,8 @@
     for d in range(1, n):
         label_copy(d).start()
     wave_copy.wait()
+    for copy in in_copies:
+        copy.wait()
 
     for s in range(sectors):
         wave = jnp.concatenate([wave_all[0, s], wave_all[1, s]], axis=-1)
@@ -155,7 +175,8 @@
             ).astype(jnp.bfloat16)
     chain[pairs] = jnp.zeros((rows, width), jnp.float32)
 
-    def compute(r):
+    def compute(u):
+        r, t = u // parts, u % parts
         def body(ks, carry):
             k = ks // sectors
             right = prods[ks]
@@ -163,7 +184,7 @@
                 p = ks * outs + m
                 b = lidx_ref[p]
                 left = left_all[r][(b // blocks) * per + k * blocks + lax.rem(b, blocks)]
-                value = jnp.dot(left.reshape(rows, -1), right, preferred_element_type=jnp.float32)
+                value = jnp.dot(left.reshape(rows * parts, -1)[t * rows : (t + 1) * rows], right, preferred_element_type=jnp.float32)
                 chain[p] = value + chain[prev_s[p]]
             return carry
 
@@ -221,27 +242,26 @@
                 total = total + env_all[r][e, l].astype(jnp.float32)
             out_ref[l, r * rows : (r + 1) * rows] = total
 
+    summed = 0
     for r in range(chunks):
         relay(r)
         if r + 1 < chunks:
             begin(r + 1)
         gathered(r)
         own_copies[r].wait()
-        compute(r)
-        send_slots(r)
-        if r == 1:
+        for u in range(r * parts, (r + 1) * parts):
+            compute(u)
+            send_slots(u)
+        if r == 0:
             for d in range(1, n):
                 label_copy(d).wait_recv()
-        if r >= 1:
-            sum_slots(r - 1)
-        if r >= 2:
-            finish(r - 2)
-    if chunks == 1:
-        for d in range(1, n):
-            label_copy(d).wait_recv()
-    sum_slots(chunks - 1)
-    for r in range(max(chunks - 2, 0), chunks):
-        finish(r)
+        while summed < r * parts:
+            sum_slots(summed)
+            summed += 1
+    for u in range(summed, units):
+        sum_slots(u)
+    for u in range(units):
+        finish(u)
 
     for r in range(chunks):
         for s in range(n - 1):
@@ -254,9 +274,11 @@
                 hop(r, s, False, me + s).wait_send()
         for d in range(1, n):
             sibling(r, lax.rem(me + d, n), core).wait_send()
-            slot_copy(r, d).wait_send()
+    for u in range(units):
+        for d in range(1, n):
+            slot_copy(u, d).wait_send()
         for d in range(1, n_env):
-            env_copy(r, d).wait_send()
+            env_copy(u, d).wait_send()
     for d in range(1, n):
         label_copy(d).wait_send()
 
@@ -266,40 +288,48 @@
     terms, blocks = left_env.shape[:2]
     outs = left_index.shape[-1]
     chunks = CHUNKS
-    rows = height // chunks
+    parts = PARTS
+    units = chunks * parts
+    span = height // chunks
+    rows = span // parts
     pairs = terms * sectors * outs
     per = terms * blocks
     bf16, f32 = jnp.bfloat16, jnp.float32
-    left = left_env.reshape(per, chunks, 2, rows // 2, height)
+    left = left_env.reshape(per, chunks, 2, span // 2, height)
     vmem = pl.BlockSpec(memory_space=pltpu.VMEM)
-    smem = pl.BlockSpec(memory_space=pltpu.SMEM)
+    hbm = pl.BlockSpec(memory_space=pltpu.HBM)
     dma = pltpu.SemaphoreType.DMA
     scratch = [
         pltpu.VMEM((2, sectors, height, width), bf16),
+        pltpu.VMEM(right_env.shape, bf16),
         pltpu.VMEM((terms * sectors, height, width), bf16),
         pltpu.VMEM((pairs + 1, rows, width), f32),
         pltpu.VMEM((n, SLOTS, 8, 128), jnp.int32),
         pltpu.VMEM((n, SLOTS, 8, 128), jnp.int32),
-        pltpu.VMEM((chunks, sectors, rows, width), f32),
+        pltpu.VMEM((units, sectors, rows, width), f32),
         pltpu.SMEM((pairs,), jnp.int32),
         pltpu.SMEM((n * sectors,), jnp.int32),
+        pltpu.SMEM(left_index.shape, jnp.int32),
+        pltpu.SMEM(left_index.shape, jnp.int32),
+        pltpu.SMEM((pairs,), jnp.int32),
+        pltpu.SMEM((pairs,), jnp.int32),
     ]
-    scratch += [pltpu.VMEM((n * per, 2, rows // 2, height), bf16)] * chunks
-    scratch += [pltpu.VMEM((n * SLOTS, rows, width), bf16)] * (2 * chunks)
-    scratch += [pltpu.VMEM((n_env, sectors, rows, width), bf16)] * chunks
+    scratch += [pltpu.VMEM((n * per, 2, span // 2, height), bf16)] * chunks
+    scratch += [pltpu.VMEM((n * SLOTS, rows, width), bf16)] * (2 * units)
+    scratch += [pltpu.VMEM((n_env, sectors, rows, width), bf16)] * units
     scratch += [dma((chunks, n - 1))] * 4 + [dma((chunks, n))] * 2 + [dma, dma]
-    scratch += [dma((chunks, n))] * 2 + [dma((n,))] * 2 + [dma((chunks, n_env))] * 2 + [dma((chunks,))]
-    dims = (n, n_env, chunks, terms, sectors, blocks, outs)
+    scratch += [dma((units, n))] * 2 + [dma((n,))] * 2 + [dma((units, n_env))] * 2 + [dma((chunks + 4,))]
+    dims = (n, n_env, chunks, parts, terms, sectors, blocks, outs)
     return pl.pallas_call(
         functools.partial(kernel, dims),
         out_shape=jax.ShapeDtypeStruct(wavefunction.shape, f32),
-        in_specs=[vmem, vmem, vmem, smem, smem],
+        in_specs=[hbm] * 5,
         out_specs=vmem,
         scratch_shapes=scratch,
         compiler_params=pltpu.CompilerParams(
-            collective_id=0, has_side_effects=True, vmem_limit_bytes=48 * 1024 * 1024
+            collective_id=0, has_side_effects=True, vmem_limit_bytes=63 * 1024 * 1024
         ),
-    )(wavefunction, left, right_env, left_index.reshape(-1), out_sector.reshape(-1))
+    )(wavefunction, left, right_env, left_index, out_sector)
 
 
 def solution(mesh):

time: 55.7 us -> 47.5 us (0.85)
  Pallas kernels: 50.7 us -> 45.4 us
  local copies, waits for them, and re-layouts: 4.7 us -> 1.87 us
    pallas_call x1, Pallas kernels: 50.7 us -> 45.4 us  [on_device(): pl.pallas_call(functools.partial(kernel, dims), out_shape=jax.ShapeDtypeS...]
    unnamed x9 -> x1, local copies, waits for them, and re-layouts: 3.84 us -> 1.87 us
    reshape x2 -> x0, local copies, waits for them, and re-layouts: 0.87 us -> none  [the longest x1 0.78 us: on_device(): left_index.reshape(-1)]
where the time goes in v2:
time: 47.5 us; the launch traced here: 47.3 us
  Pallas kernels  45.4 us (96%)
  local copies, waits for them, and re-layouts  1.87 us (4%)
    pallas_call x1, Pallas kernels, on_device(): pl.pallas_call(functools.partial(kernel, dims), out_shape=jax.ShapeDtypeS...  45.4 us
    unnamed x1, local copies, waits for them, and re-layouts  1.87 us

profile of v2, /device:TPU:0, one launch (start us, length us, event | category | flops | bytes accessed | tf_op | source)
XLA Modules:
  0.0 47.3 jit_solution(11316359207181291751)
XLA Ops:
  0.0 45.4 %shard_map.55 = f32[4,256,128]{2,1,0:T(8,128)} custom-call(bf16[4,256,128]{2,1,0:T(8,128)(2,1)} %refs_0_.1, bf16[4,1,2,128,256]{4,3,2,1,0:T(8,128)(2,1)} %bitcast.1, bf16[2,4,128,256]{3,2,1,0:T(8,128)(2,1)} %refs_2_.1, s32[2,4,6]{2,1,0:T(4,128)} %refs_3_.1, s32[2,4,6]{2,1,0:T(4,128)} %refs_4_.1), custom_call_target="tpu_custom_call" | custom-call | tf_op jit(solution)/shard_map/pallas_call | solution.py:323
  45.4 1.9 %copy.7 = f32[4,256,128]{2,1,0:T(8,128)} copy(f32[4,256,128]{2,1,0:T(8,128)} %shard_map.55) | data formatting | bytes 1048576

commit v3 on v2

--- a/solution.py
+++ b/solution.py
@@ -11,6 +11,7 @@
 SLOTS = 2
 CHUNKS = 1
 PARTS = 4
+PIECES = 2
 
 
 def kernel(dims, *refs):
@@ -47,53 +48,55 @@
             src_ref=src, dst_ref=dst, send_sem=send, recv_sem=recv, device_id=where, device_id_type=MESH
         )
 
-    def piece(r, origin):
-        return left_all[r].at[pl.ds(origin * per, per), core]
-
-    def hop(r, s, up, origin):
-        src = left_ref.at[:, r, core] if s == 0 else piece(r, origin)
+    part = per // PIECES
+
+    def piece(r, q, origin):
+        return left_all[r].at[pl.ds(origin * per + q * part, part), core]
+
+    def hop(r, q, s, up, origin):
+        src = left_ref.at[pl.ds(q * part, part), r, core] if s == 0 else piece(r, q, origin)
         send, recv = (up_s, up_r) if up else (dn_s, dn_r)
         where = jnp.minimum(me + 1, n - 1) if up else jnp.maximum(me - 1, 0)
-        return remote(src, piece(r, origin), send.at[r, s], recv.at[r, s], {"sec": where})
-
-    def sibling(r, origin, half):
-        ref = left_all[r].at[pl.ds(origin * per, per), half]
-        return remote(ref, ref, sib_s.at[r, origin], sib_r.at[r, origin], {"rep": 1 - core})
+        return remote(src, piece(r, q, origin), send.at[r * PIECES + q, s], recv.at[r * PIECES + q, s], {"sec": where})
+
+    def sibling(r, q, origin, half):
+        ref = left_all[r].at[pl.ds(origin * per + q * part, part), half]
+        at = r * PIECES + q
+        return remote(ref, ref, sib_s.at[at, origin], sib_r.at[at, origin], {"rep": 1 - core})
 
     def begin(r):
         @pl.when(me + 1 < n)
         def _():
-            hop(r, 0, True, me).start()
+            for q in range(PIECES):
+                hop(r, q, 0, True, me).start()
 
         @pl.when(me > 0)
         def _():
-            hop(r, 0, False, me).start()
+            for q in range(PIECES):
+                hop(r, q, 0, False, me).start()
+
+    def pass_on(r, q, s, up):
+        origin = me - 1 - s if up else me + 1 + s
+
+        @pl.when((origin >= 0) & (origin <= n - 1))
+        def _():
+            hop(r, q, s, up, origin).wait_recv()
+            if s + 1 <= n - 2:
+                @pl.when((me + 1 < n) if up else (me > 0))
+                def _():
+                    hop(r, q, s + 1, up, origin).start()
+            sibling(r, q, origin, core).start()
 
     def relay(r):
         for s in range(n - 1):
-            @pl.when(me - 1 - s >= 0)
-            def _():
-                origin = me - 1 - s
-                hop(r, s, True, origin).wait_recv()
-                if s + 1 <= n - 2:
-                    @pl.when(me + 1 < n)
-                    def _():
-                        hop(r, s + 1, True, origin).start()
-                sibling(r, origin, core).start()
-
-            @pl.when(me + 1 + s <= n - 1)
-            def _():
-                origin = me + 1 + s
-                hop(r, s, False, origin).wait_recv()
-                if s + 1 <= n - 2:
-                    @pl.when(me > 0)
-                    def _():
-                        hop(r, s + 1, False, origin).start()
-                sibling(r, origin, core).start()
+            for q in range(PIECES):
+                pass_on(r, q, s, True)
+                pass_on(r, q, s, False)
 
     def gathered(r):
         for d in range(1, n):
-            sibling(r, lax.rem(me + d, n), 1 - core).wait_recv()
+            for q in range(PIECES):
+                sibling(r, q, lax.rem(me + d, n), 1 - core).wait_recv()
 
     begin(0)
     wave_copy = remote(wave_ref, wave_all.at[core], w_s, w_r, {"rep": 1 - core})
@@ -180,12 +183,15 @@
         def body(ks, carry):
             k = ks // sectors
             right = prods[ks]
+            lefts = []
+            for m in range(outs):
+                b = lidx_ref[ks * outs + m]
+                left = left_all[r][(b // blocks) * per + k * blocks + lax.rem(b, blocks)]
+                lefts.append(left.reshape(rows * parts, -1)[t * rows : (t + 1) * rows])
+            values = jnp.dot(jnp.concatenate(lefts, axis=0), right, preferred_element_type=jnp.float32)
             for m in range(outs):
                 p = ks * outs + m
-                b = lidx_ref[p]
-                left = left_all[r][(b // blocks) * per + k * blocks + lax.rem(b, blocks)]
-                value = jnp.dot(left.reshape(rows * parts, -1)[t * rows : (t + 1) * rows], right, preferred_element_type=jnp.float32)
-                chain[p] = value + chain[prev_s[p]]
+                chain[p] = values[m * rows : (m + 1) * rows] + chain[prev_s[p]]
             return carry
 
         lax.fori_loop(0, terms * sectors, body, 0)
@@ -201,7 +207,7 @@
         )
 
     def send_slots(r):
-        for d in range(n - 1, 0, -1):
+        for d in range(1, n):
             owner = lax.rem(me + d, n)
             for i in range(SLOTS):
                 slot_send[r][owner * SLOTS + i] = chain[slot_of(owner, i)[1]].astype(jnp.bfloat16)
@@ -216,8 +222,10 @@
 
     def env_copy(r, d):
         peer = lax.rem(env + d, n_env)
-        ref = env_all[r].at[env]
-        return remote(ref, ref, ev_s.at[r, d], ev_r.at[r, d], {"env": peer})
+        return remote(env_all[r], out_ref.at[env, :, pl.ds(r * rows, rows)], ev_s.at[r, d], ev_r.at[r, d], {"env": peer})
+
+    def own_part(r):
+        return pltpu.make_async_copy(env_all[r], out_ref.at[env, :, pl.ds(r * rows, rows)], ev_s.at[r, 0])
 
     def sum_slots(r):
         for d in range(1, n):
@@ -229,18 +237,15 @@
                 for i in range(SLOTS):
                     mask = lab_recv[source, i][:1] == l
                     total = total + jnp.where(mask, slot_recv[r][source * SLOTS + i].astype(jnp.float32), 0.0)
-            env_all[r][env, l] = total.astype(env_all[r].dtype)
+            env_all[r][l] = total.astype(env_all[r].dtype)
         for d in range(1, n_env):
             env_copy(r, d).start()
+        own_part(r).start()
 
     def finish(r):
         for d in range(1, n_env):
             env_copy(r, d).wait_recv()
-        for l in range(sectors):
-            total = env_all[r][0, l].astype(jnp.float32)
-            for e in range(1, n_env):
-                total = total + env_all[r][e, l].astype(jnp.float32)
-            out_ref[l, r * rows : (r + 1) * rows] = total
+        own_part(r).wait()
 
     summed = 0
     for r in range(chunks):
@@ -267,13 +272,16 @@
         for s in range(n - 1):
             @pl.when((me - s >= 0) & (me + 1 < n))
             def _():
-                hop(r, s, True, me - s).wait_send()
+                for q in range(PIECES):
+                    hop(r, q, s, True, me - s).wait_send()
 
             @pl.when((me + s <= n - 1) & (me > 0))
             def _():
-                hop(r, s, False, me + s).wait_send()
-        for d in range(1, n):
-            sibling(r, lax.rem(me + d, n), core).wait_send()
+                for q in range(PIECES):
+                    hop(r, q, s, False, me + s).wait_send()
+        for d in range(1, n):
+            for q in range(PIECES):
+                sibling(r, q, lax.rem(me + d, n), core).wait_send()
     for u in range(units):
         for d in range(1, n):
             slot_copy(u, d).wait_send()
@@ -296,7 +304,6 @@
     per = terms * blocks
     bf16, f32 = jnp.bfloat16, jnp.float32
     left = left_env.reshape(per, chunks, 2, span // 2, height)
-    vmem = pl.BlockSpec(memory_space=pltpu.VMEM)
     hbm = pl.BlockSpec(memory_space=pltpu.HBM)
     dma = pltpu.SemaphoreType.DMA
     scratch = [
@@ -316,20 +323,24 @@
     ]
     scratch += [pltpu.VMEM((n * per, 2, span // 2, height), bf16)] * chunks
     scratch += [pltpu.VMEM((n * SLOTS, rows, width), bf16)] * (2 * units)
-    scratch += [pltpu.VMEM((n_env, sectors, rows, width), bf16)] * units
-    scratch += [dma((chunks, n - 1))] * 4 + [dma((chunks, n))] * 2 + [dma, dma]
+    scratch += [pltpu.VMEM((sectors, rows, width), bf16)] * units
+    scratch += [dma((chunks * PIECES, n - 1))] * 4 + [dma((chunks * PIECES, n))] * 2 + [dma, dma]
     scratch += [dma((units, n))] * 2 + [dma((n,))] * 2 + [dma((units, n_env))] * 2 + [dma((chunks + 4,))]
     dims = (n, n_env, chunks, parts, terms, sectors, blocks, outs)
-    return pl.pallas_call(
+    sums = pl.pallas_call(
         functools.partial(kernel, dims),
-        out_shape=jax.ShapeDtypeStruct(wavefunction.shape, f32),
+        out_shape=jax.ShapeDtypeStruct((n_env,) + wavefunction.shape, bf16),
         in_specs=[hbm] * 5,
-        out_specs=vmem,
+        out_specs=hbm,
         scratch_shapes=scratch,
         compiler_params=pltpu.CompilerParams(
             collective_id=0, has_side_effects=True, vmem_limit_bytes=63 * 1024 * 1024
         ),
     )(wavefunction, left, right_env, left_index, out_sector)
+    product = sums[0].astype(f32)
+    for e in range(1, n_env):
+        product = product + sums[e].astype(f32)
+    return product
 
 
 def solution(mesh):

time: 47.5 us -> 43.7 us (0.920)
  Pallas kernels: 45.4 us -> 41.6 us
  other arithmetic: 0 us -> 1.88 us
  local copies, waits for them, and re-layouts: 1.87 us -> 0 us
    pallas_call x1, Pallas kernels: 45.4 us -> 41.6 us  [on_device(): pl.pallas_call(functools.partial(kernel, dims), out_shape=jax.ShapeDtypeS...]
    add x0 -> x1, other arithmetic: none -> 1.88 us  [on_device(): product = product + sums[e].astype(f32)]
    unnamed x1 -> x0, local copies, waits for them, and re-layouts: 1.87 us -> none
where the time goes in v3:
time: 43.7 us; the launch traced here: 43.5 us
  Pallas kernels  41.6 us (95%)
  other arithmetic  1.88 us (4%)
    pallas_call x1, Pallas kernels, on_device(): pl.pallas_call(functools.partial(kernel, dims), out_shape=jax.ShapeDtypeS...  41.6 us
    add x1, other arithmetic, on_device(): product = product + sums[e].astype(f32)  1.88 us

profile of v3, /device:TPU:0, one launch (start us, length us, event | category | flops | bytes accessed | tf_op | source)
XLA Modules:
  0.0 43.5 jit_solution(4393815058161280093)
XLA Ops:
  0.0 41.6 %shard_map.55 = bf16[2,4,256,128]{3,2,1,0:T(8,128)(2,1)} custom-call(bf16[4,256,128]{2,1,0:T(8,128)(2,1)} %refs_0_.1, bf16[4,1,2,128,256]{4,3,2,1,0:T(8,128)(2,1)} %bitcast.3, bf16[2,4,128,256]{3,2,1,0:T(8,128)(2,1)} %refs_2_.1, s32[2,4,6]{2,1,0:T(4,128)} %refs_3_.1, s32[2,4,6]{2,1,0:T(4,128)} %refs_4_.1), custom_call_target="tpu_custom_call" | custom-call | tf_op jit(solution)/shard_map/pallas_call | solution.py:330
  41.6 1.9 %add_bitcast_fusion = f32[4,256,128]{2,1,0:T(8,128)} fusion(bf16[2,4,256,128]{3,2,1,0:T(8,128)(2,1)} %shard_map.55), kind=kLoop, calls=%fused_computation | loop fusion | flops 393216 | bytes 1048576 | tf_op jit(solution)/shard_map/add | solution.py:342
